TPU v7x, 32 devices: a whole 2x2x4 slice. The times are simulated.
32 devices in a mesh: snap: 4 (over y, x), plane: 8 (over z, core).
Axes of the slice: x: 2, y: 2, z: 4, core: 2. Of those that a mesh axis runs over, the one named last changes fastest.
Arguments:
- velocity: bfloat16 [4, 32, 3, 128, 128], P('snap', 'plane'), may hold values from -6 to 6
- plane_count: int32 [8], P('plane'), may hold values from 1 to 4, as said below
- inv_span: float32 [8, 4], P('plane'), may hold values from 0.5 to 4
- kernels: float32 [3, 2, 3, 3], replicated, may hold values from -2.4 to 2.4
- omega_block: int32 [8, 4], P('plane'), may hold values from 0 to 7
- omega_table: bfloat16 [8, 9, 32, 256], replicated, may hold values from -0.0625 to 0.0625
- omega_stream: bfloat16 [32, 256], replicated, may hold values from -6 to 6
- wall_shear: bfloat16 [4, 2, 128, 128], P('snap', None, 'plane'), may hold values from -6 to 6
Outputs:
- sketch: float32 [2, 32, 32, 256], P(None, 'plane', 'snap')
- gram: float32 [256, 256], replicated
Inputs may be any that keep to these rules, and one draw needn't show every extreme that they name: `plane_count`: every index of plane holds 1 or more live slots, slots 0 onwards; some index holds 4.
All inputs are finite; a program needn't handle non-finite values.
Results may differ from a plain program's by a relative error of at most 0.0043.
Values may be sent and summed in bfloat16 or wider, within the bound.
A program may use at most 64 MiB of HBM per device.

v0:
```python
import jax
import jax.numpy as jnp
from jax import lax
from jax.sharding import PartitionSpec as P

X = 128
ZW = 128


def shifted(value, axis, steps):
    count = lax.axis_size(axis)
    leading, last = (max(0, -steps), min(count, count - steps))
    return lax.ppermute(value, axis, [(source, source + steps) for source in range(leading, last)])


def in_plane(centre, kernels):
    snaps, comps, zw, xw = centre.shape
    field = centre.astype(jnp.float32)
    padded = jnp.pad(field, ((0, 0), (0, 0), (1, 1), (1, 1)))
    first = jnp.zeros_like(field)
    second = jnp.zeros_like(field)
    for row_a in range(3):
        for col_b in range(3):
            window = padded[:, :, row_a : row_a + zw, col_b : col_b + xw]
            first = first + kernels[:, 0, row_a, col_b][None, :, None, None] * window
            second = second + kernels[:, 1, row_a, col_b][None, :, None, None] * window
    return (first, second)


def features(centre, below, above, span, kernels):
    snaps, comps, zw, xw = centre.shape
    first, second = in_plane(centre, kernels)
    normal = (above.astype(jnp.float32) - below.astype(jnp.float32)) * span
    grads = jnp.stack([first, second, normal], axis=2).reshape(snaps, 9, zw, xw)
    filtered = grads.reshape(snaps, 9, zw // 4, 4, xw // 4, 4).mean(axis=(3, 5))
    return filtered.astype(jnp.bfloat16)


def per_device(
    velocity, plane_count, inv_span, kernels, omega_block, omega_table, omega_stream, wall_shear
):
    slots = velocity.shape[1]
    live_count = plane_count[0]
    coef = jnp.zeros((velocity.shape[0], omega_stream.shape[1]), jnp.float32)
    last_live = lax.dynamic_index_in_dim(velocity, live_count - 1, 1, keepdims=False)
    from_below = shifted(last_live, "plane", 1)
    from_above = shifted(velocity[:, 0], "plane", -1)
    for slot in range(slots):
        below = from_below if slot == 0 else velocity[:, slot - 1]
        if slot + 1 < slots:
            above = jnp.where(slot + 1 < live_count, velocity[:, slot + 1], from_above)
        else:
            above = from_above
        feats = features(velocity[:, slot], below, above, inv_span[0, slot], kernels)
        proj = jnp.einsum("sczx,xk->sczk", feats, omega_stream, preferred_element_type=jnp.float32)
        table = lax.dynamic_index_in_dim(
            omega_table, omega_block[0, slot], 0, keepdims=False
        ).astype(jnp.float32)
        term = jnp.einsum("sczk,czk->sk", proj, table, precision=lax.Precision.HIGHEST)
        coef = coef + jnp.where(slot < live_count, term, jnp.zeros_like(term))
    coef = lax.psum(coef, "plane")
    snaps, comps, zw, xw = wall_shear.shape
    shear_f = (
        wall_shear.astype(jnp.float32)
        .reshape(snaps, comps, zw // 4, 4, xw // 4, 4)
        .mean(axis=(3, 5))
    )
    partial_sketch = jnp.einsum("smzx,sk->mzxk", shear_f, coef, precision=lax.Precision.HIGHEST)
    sketch = lax.psum_scatter(partial_sketch, "snap", scatter_dimension=2, tiled=True)
    total_rows = 2 * (X // 4) * (ZW // 4)
    all_shear, all_coef = (
        lax.all_gather(shear_f, "snap", axis=0, tiled=True),
        lax.all_gather(coef, "snap", axis=0, tiled=True),
    )
    shear_rows = all_shear.reshape(all_shear.shape[0], -1)
    local_inner = jnp.dot(shear_rows, shear_rows.T, precision=lax.Precision.HIGHEST)
    inner = lax.psum(local_inner, "plane")
    weighted = jnp.dot(inner, all_coef, precision=lax.Precision.HIGHEST)
    gram = jnp.dot(all_coef.T, weighted, precision=lax.Precision.HIGHEST) / jnp.float32(total_rows)
    return (sketch, gram)


def solution(mesh):
    return jax.shard_map(
        per_device,
        mesh=mesh,
        in_specs=(
            P("snap", "plane", None, None, None),
            P("plane"),
            P("plane", None),
            P(),
            P("plane", None),
            P(),
            P(),
            P("snap", None, "plane", None),
        ),
        out_specs=(P(None, "plane", "snap", None), P()),
        check_vma=False,
    )
```

profile of v0, /device:TPU:0, one launch (start us, length us, event | category | flops | bytes accessed | tf_op | source)
XLA Modules:
  0.0 198.5 jit_solution(6015031213508847965)
XLA Ops:
  7.9 1.2 fusion.26
  9.1 1.3 collective-permute-start
  10.4 3.0 %collective-permute-start.1 = (bf16[1,3,128,128]{3,2,1,0:T(8,128)(2,1)S(1)}, bf16[1,3,128,128]{3,2,1,0:T(8,128)(2,1)S(1)}, u32[]{:S(2)}, u32[]{:S(2)}) collective-permute-start(bf16[1,3,128,128]{3,2,1,0:T(8,128)(2,1)S(1)} %get-tuple-element.30), channel_id=1, source_target_pairs={{0,1},{1,2},{2,3},{3,4},{4,5},{5,6},{6,7},{8,9},{9,10},{10,11},{11... | collective-permute-start | bytes 294920 | tf_op jit(solution)/shard_map/ppermute | solution.py:13
  13.4 0.7 fusion.28
  19.2 0.2 slice_reduce_fusion.17
  19.5 0.5 reshape.265
  20.1 9.6 %all-gather = f32[8,4,32]{2,1,0:T(4,128)S(1)} all-gather(f32[2,4,32]{2,1,0:T(4,128)S(1)} %broadcast_multiply_fusion.1), channel_id=2, replica_groups=mesh['snap'=4,'plane'=8] {'snap'}, dimensions={0}, use_global_device_ids=true | all-gather | bytes 5120 | tf_op jit(solution)/shard_map/all_gather | solution.py:72
  32.5 1.3 add_bitcast_fusion.7
  33.8 1.3 add_bitcast_fusion.6
  35.2 0.7 fusion.27
  35.9 2.7 %multiply_bitcast_fusion.3 = (f32[1,3,1,128,128]{4,3,1,2,0:T(8,128)S(1)}, f32[1,3,1,128,128]{4,3,1,2,0:T(8,128)S(1)}, f32[1,3,1,128,128]{4,3,1,2,0:T(8,128)S(1)}, f32[1,3,1,128,128]{4,3,1,2,0:T(8,128)S(1)}) fusion(bf16[1,3,128,128]{3,2,1,0:T(8,128)(2,1)S(1)} %collective-permute-done.1, bf16[1,3,128,128]{3,2,1,0:T(8,128)(2,1)S(1)} %collective-permute-done, ...), kind=kLoop, calls=%fused_computation.59 | loop fusion | flops 933888 | bytes 1376275 | tf_op jit(solution)/shard_map/stack | solution.py:34
  38.7 21.0 %reshape_reshape.12 = f32[9,32,4,32,4]{4,3,2,1,0:T(8,128)} reshape(f32[1,3,3,128,128]{4,3,2,1,0:T(8,128)S(1)} %copy.18) | data formatting | bytes 1179648 | tf_op jit(solution)/shard_map/reshape;reshape | solution.py:35
  59.7 7.9 %reduce_sum.46 = f32[9,32,32]{2,1,0:T(8,128)S(1)} reduce(f32[9,32,4,32,4]{4,3,2,1,0:T(8,128)} %reshape_reshape.12, f32[]{:T(128)} %constant.38.clone.1), dimensions={2,4}, to_apply=%region_1.2 | reduce | flops 138240 | bytes 626692 | tf_op jit(solution)/shard_map/reduce_sum | solution.py:35
  67.7 20.8 %reshape_reshape.13 = f32[9,32,4,32,4]{4,3,2,1,0:T(8,128)} reshape(f32[1,3,3,128,128]{4,3,2,1,0:T(8,128)S(1)} %copy.19) | data formatting | bytes 1179648 | tf_op jit(solution)/shard_map/reshape;reshape | solution.py:35
  88.5 7.9 %reduce_sum.47 = f32[9,32,32]{2,1,0:T(8,128)S(1)} reduce(f32[9,32,4,32,4]{4,3,2,1,0:T(8,128)} %reshape_reshape.13, f32[]{:T(128)} %constant.38.clone.1), dimensions={2,4}, to_apply=%region_2.3 | reduce | flops 138240 | bytes 626692 | tf_op jit(solution)/shard_map/reduce_sum | solution.py:35
  96.6 20.8 %reshape_reshape.14 = f32[9,32,4,32,4]{4,3,2,1,0:T(8,128)} reshape(f32[1,3,3,128,128]{4,3,2,1,0:T(8,128)S(1)} %copy.20) | data formatting | bytes 1179648 | tf_op jit(solution)/shard_map/reshape;reshape | solution.py:35
  117.4 7.9 %reduce_sum.48 = f32[9,32,32]{2,1,0:T(8,128)S(1)} reduce(f32[9,32,4,32,4]{4,3,2,1,0:T(8,128)} %reshape_reshape.14, f32[]{:T(128)} %constant.38.clone.1), dimensions={2,4}, to_apply=%region_3.4 | reduce | flops 138240 | bytes 626692 | tf_op jit(solution)/shard_map/reduce_sum | solution.py:35
  125.4 20.8 %reshape_reshape.15 = f32[9,32,4,32,4]{4,3,2,1,0:T(8,128)} reshape(f32[1,3,3,128,128]{4,3,2,1,0:T(8,128)S(1)} %copy.21) | data formatting | bytes 1179648 | tf_op jit(solution)/shard_map/reshape;reshape | solution.py:35
  146.2 8.0 %reduce_sum.49 = f32[9,32,32]{2,1,0:T(8,128)S(1)} reduce(f32[9,32,4,32,4]{4,3,2,1,0:T(8,128)} %reshape_reshape.15, f32[]{:T(128)} %constant.38.clone.1), dimensions={2,4}, to_apply=%region_4.5 | reduce | flops 138240 | bytes 626692 | tf_op jit(solution)/shard_map/reduce_sum | solution.py:35
  155.1 14.2 %all-reduce.4 = (f32[1,256]{1,0:T(1,128)S(1)}, f32[4,4]{1,0:T(4,128)S(1)}) all-reduce(f32[1,256]{1,0:T(1,128)S(1)} %bitcast.142, f32[4,4]{1,0:T(4,128)S(1)} %convolution_bitcast_fusion.4), channel_id=1, replica_groups=mesh['snap'=4,'plane'=8] {'plane'}, use_global_device_ids=true, to_apply=%region_5.6 | all-reduce | flops 272 | bytes 2176 | tf_op jit(solution)/shard_map/psum | solution.py:61
  169.3 0.8 broadcast_multiply_fusion
  170.1 8.0 %all-gather.1 = f32[4,1,256]{2,1,0:T(1,128)S(1)} all-gather(f32[1,1,256]{2,1,0:T(1,128)S(1)} %bitcast.141), channel_id=1, replica_groups=mesh['snap'=4,'plane'=8] {'snap'}, dimensions={0}, use_global_device_ids=true | all-gather | bytes 5120 | tf_op jit(solution)/shard_map/all_gather | solution.py:73
  178.2 1.2 convolution_multiply_fusion
  179.4 12.3 %reduce-scatter.2.cloned.1.call-done = f32[2,4,8,256]{3,2,1,0:T(8,128)} async-done(((f32[2,4,32,256]{3,2,1,0:T(8,128)}), f32[2,4,8,256]{3,2,1,0:T(8,128)}) %reduce-scatter.2.cloned.1.call-update) | async-done | bytes 65552 | tf_op jit(solution)/shard_map/reduce_scatter | solution.py:69
  (34 shorter events, 1.6 us)
Async XLA Ops:
  7.2 147.1 %copy-start = (bf16[32,256]{1,0:T(8,128)(2,1)S(1)}, bf16[32,256]{1,0:T(8,128)(2,1)}, u32[]{:S(2)}) copy-start(bf16[32,256]{1,0:T(8,128)(2,1)} %param.14) | copy-start | bytes 49156
  7.2 6.3 %copy-start.5 = (s32[1,4]{1,0:T(1,128)S(1)}, s32[1,4]{1,0:T(1,128)}, u32[]{:S(2)}) copy-start(s32[1,4]{1,0:T(1,128)} %param.12) | copy-start | bytes 52
  7.2 12.0 %copy-start.3 = (f32[3,2,3,3]{3,1,2,0:T(2,128)S(1)}, f32[3,2,3,3]{3,1,2,0:T(2,128)}, u32[]{:S(2)}) copy-start(f32[3,2,3,3]{3,1,2,0:T(2,128)} %param.11) | copy-start | bytes 652
  7.2 12.3 %copy-start.4 = (bf16[1,2,16,128]{3,2,1,0:T(8,128)(2,1)S(1)}, bf16[1,2,16,128]{3,2,1,0:T(8,128)(2,1)}, u32[]{:S(2)}) copy-start(bf16[1,2,16,128]{3,2,1,0:T(8,128)(2,1)} %param.15) | copy-start | bytes 24580
  7.2 184.5 %reduce-scatter.2.cloned.1.call-start = ((), (), s32[]{:S(2)}) async-start(), calls=%async_computation.1 | async-start | bytes 327680 | tf_op jit(solution)/shard_map/reduce_scatter | solution.py:69
  9.1 26.8 %collective-permute-start = (bf16[1,3,128,128]{3,2,1,0:T(8,128)(2,1)S(1)}, bf16[1,3,128,128]{3,2,1,0:T(8,128)(2,1)S(1)}, u32[]{:S(2)}, u32[]{:S(2)}) collective-permute-start(bf16[1,3,128,128]{3,2,1,0:T(8,128)(2,1)S(1)} %get-tuple-element.31), channel_id=1, source_target_pairs={{1,0},{2,1},{3,2},{4,3},{5,4},{6,5},{7,6},{9,8},{10,9},{11,10},{12... | collective-permute-start | bytes 294920 | tf_op jit(solution)/shard_map/ppermute | solution.py:13
  10.4 25.5 %collective-permute-start.1 = (bf16[1,3,128,128]{3,2,1,0:T(8,128)(2,1)S(1)}, bf16[1,3,128,128]{3,2,1,0:T(8,128)(2,1)S(1)}, u32[]{:S(2)}, u32[]{:S(2)}) collective-permute-start(bf16[1,3,128,128]{3,2,1,0:T(8,128)(2,1)S(1)} %get-tuple-element.30), channel_id=1, source_target_pairs={{0,1},{1,2},{2,3},{3,4},{4,5},{5,6},{6,7},{8,9},{9,10},{10,11},{11... | collective-permute-start | bytes 294920 | tf_op jit(solution)/shard_map/ppermute | solution.py:13
  33.8 1.4 copy-start.6
  33.8 2.0 %copy-start.1 = (bf16[1,4,3,128,128]{4,3,2,1,0:T(8,128)(2,1)S(1)}, bf16[1,4,3,128,128]{4,3,2,1,0:T(8,128)(2,1)}, u32[]{:S(2)}) copy-start(bf16[1,4,3,128,128]{4,3,2,1,0:T(8,128)(2,1)} %param.8) | copy-start | bytes 1179652
  146.2 8.0 %copy-start.2 = (bf16[8,9,32,256]{3,2,1,0:T(8,128)(2,1)S(1)}, bf16[8,9,32,256]{3,2,1,0:T(8,128)(2,1)}, u32[]{:S(2)}) copy-start(bf16[8,9,32,256]{3,2,1,0:T(8,128)(2,1)} %param.13) | copy-start | bytes 3538948
Sparse Core Ops, SparseCore 0:
  170.2 21.4 reduce-scatter.1
where the time goes:
time: 199 us
  local copies, waits for them, and re-layouts  85.9 us (43%)
  other arithmetic  39.3 us (20%)
  blocking collectives  31.8 us (16%)
  between operations  22.6 us (11%)
  waiting for transfers between devices  12.3 us (6%)
  starting transfers between devices  4.37 us (2%)
  matrix products  2.22 us (1%)
    another operation x4, local copies, waits for them, and re-layouts, features(): filtered = grads.reshape(snaps, 9, zw // 4, 4, xw // 4, 4).mean(axis=(3, 5))  83.6 us
    reduce_sum x4, other arithmetic, features(): filtered = grads.reshape(snaps, 9, zw // 4, 4, xw // 4, 4).mean(axis=(3, 5))  31.8 us
    psum x1, blocking collectives, per_device(): coef = lax.psum(coef, 'plane')  14.2 us
    reduce_scatter x1, waiting for transfers between devices, per_device(): lax.psum_scatter(partial_sketch, 'snap', scatter_dimension=2, tiled=True)  12.3 us
    all_gather x1, blocking collectives, per_device(): lax.all_gather(shear_f, 'snap', axis=0, tiled=True)  9.62 us
    all_gather x1, blocking collectives, per_device(): lax.all_gather(coef, 'snap', axis=0, tiled=True)  8.03 us
    another operation x5, other arithmetic, features(): grads = jnp.stack([first, second, normal], axis=2).reshape(snaps, 9, zw, xw)  5.48 us
    ppermute x2, starting transfers between devices, shifted(): lax.ppermute(value, axis, [(source, source + steps) for source in range(l...  4.33 us
  transfers between devices with their start and end apart: 3, of which 1 were waited for; matrix products, arithmetic and copies ran while one was open for 3% of the time, Pallas kernels for 0%

commit v1 on v0

v1 whole, which is shorter than its diff:
```python
import functools

import jax
import jax.numpy as jnp
from jax import lax
from jax.experimental import pallas as pl
from jax.experimental.pallas import tpu as pltpu
from jax.sharding import PartitionSpec as P

POOL = 4
MESH = pl.DeviceIdType.MESH
HIGHEST = lax.Precision.HIGHEST


def shift_rows(value, steps):
    rows = value.shape[0]
    at = lax.broadcasted_iota(jnp.int32, value.shape, 0)
    edge = 0 if steps == 1 else rows - 1
    return jnp.where(at == edge, 0.0, pltpu.roll(value, steps % rows, 0))


def kernel(
    snaps, planes,
    count_ref, span_ref, stencil_ref, block_ref, shear_ref, stream_ref, velocity_hbm, table_hbm,
    sketch_ref, gram_ref,
    velocity, table, stream, pooled, columns, feats, shear_rows, shear_all, shear_t, inner_all,
    halo_out, halo_in, coef_all, coef_snap,
    local_sem, shear_send, shear_recv, inner_send, inner_recv, halo_send, halo_recv,
    coef_send, coef_recv, snap_send, snap_recv,
):
    slots, comps, zw, xw = velocity.shape
    zf, xf = zw // POOL, xw // POOL
    width = stream_ref.shape[1]
    me_s, me_p = lax.axis_index("snap"), lax.axis_index("plane")

    get_velocity = pltpu.make_async_copy(velocity_hbm.at[0], velocity, local_sem.at[0])
    get_table = pltpu.make_async_copy(table_hbm, table, local_sem.at[1])
    get_velocity.start()
    get_table.start()

    snap_peers = [lax.rem(me_s + d, snaps) for d in range(1, snaps)]
    plane_peers = [lax.rem(me_p + d, planes) for d in range(1, planes)]
    barrier = pltpu.get_barrier_semaphore()
    for peer in snap_peers:
        pl.semaphore_signal(barrier, inc=1, device_id=(peer, me_p), device_id_type=MESH)
    for peer in plane_peers:
        pl.semaphore_signal(barrier, inc=1, device_id=(me_s, peer), device_id_type=MESH)

    row = lax.broadcasted_iota(jnp.int32, (comps * xw, xw), 0)
    lane = lax.broadcasted_iota(jnp.int32, (comps * xw, xw), 1)
    gap = lax.rem(row, xw) - POOL * lax.rem(lane, xf)
    hit = (lax.div(row, xw) == lax.div(lane, xf)) & (gap >= 0) & (gap < POOL)
    pack = jnp.where(hit, 1.0, 0.0).astype(jnp.bfloat16)
    row = lax.broadcasted_iota(jnp.int32, (xw, xw), 0)
    lane = lax.broadcasted_iota(jnp.int32, (xw, xw), 1)
    group = lax.div(lane, xf)
    gap = row - POOL * lax.rem(lane, xf) - jnp.where(group == 1, -1, jnp.where(group == 2, 1, 0))
    hit = (group < 3) & (gap >= 0) & (gap < POOL)
    shifts = jnp.where(hit, 1.0, 0.0).astype(jnp.bfloat16)

    kinds, zs = shear_ref.shape[1], shear_ref.shape[2]
    zl = zs // POOL
    shear_in = shear_ref[0].reshape(kinds * zs, xw)
    shear_rows[...] = jnp.dot(shear_in, pack[:xw], preferred_element_type=jnp.float32)
    part = [shear_rows[pl.ds(r, kinds * zl, stride=POOL), :] for r in range(POOL)]
    shear_all[me_s] = (part[0] + part[1] + part[2] + part[3]) * (1.0 / (POOL * POOL))

    pl.semaphore_wait(barrier, snaps - 1 + planes - 1)

    def send(src, dst, send_sem, recv_sem, snap, plane):
        copy = pltpu.make_async_remote_copy(
            src_ref=src, dst_ref=dst, send_sem=send_sem, recv_sem=recv_sem,
            device_id=(snap, plane), device_id_type=MESH,
        )
        copy.start()
        return copy

    shear_copies = [
        send(shear_all.at[me_s], shear_all.at[me_s], shear_send.at[d], shear_recv.at[d], peer, me_p)
        for d, peer in enumerate(snap_peers)
    ]

    get_velocity.wait()
    fields = jnp.concatenate(
        [velocity[:, i].reshape(slots * zw, xw) for i in range(comps)], axis=1
    )
    columns[pl.ds(0, slots * zw), :] = jnp.dot(fields, pack, preferred_element_type=jnp.float32)
    part = [columns[pl.ds(r, slots * zf, stride=POOL), :] for r in range(POOL)]
    pooled[...] = (part[0] + part[1] + part[2] + part[3]).reshape(slots, zf, xw)
    live_count = count_ref[0]
    halo_out[0] = pooled[0]
    last = pooled[0]
    for slot in range(1, slots):
        last = jnp.where(live_count - 1 == slot, pooled[slot], last)
    halo_out[1] = last

    def halo(which, plane):
        return pltpu.make_async_remote_copy(
            src_ref=halo_out.at[which], dst_ref=halo_in.at[which],
            send_sem=halo_send.at[which], recv_sem=halo_recv.at[which],
            device_id=(me_s, plane), device_id_type=MESH,
        )

    down = halo(0, jnp.maximum(me_p - 1, 0))
    up = halo(1, jnp.minimum(me_p + 1, planes - 1))

    @pl.when(me_p > 0)
    def _():
        down.start()

    @pl.when(me_p < planes - 1)
    def _():
        up.start()

    @pl.when(me_p == 0)
    def _():
        halo_in[1] = jnp.zeros_like(halo_in[1])

    @pl.when(me_p == planes - 1)
    def _():
        halo_in[0] = jnp.zeros_like(halo_in[0])

    for copy in shear_copies:
        copy.wait()
    every = shear_all[...]
    inner_rows = inner_all.shape[1]
    at_row = lax.broadcasted_iota(jnp.int32, (inner_rows, xw), 0)
    at_lane = lax.broadcasted_iota(jnp.int32, (inner_rows, xw), 1)
    inner = jnp.zeros((inner_rows, xw), jnp.float32)
    for a in range(snaps):
        for b in range(a, snaps):
            value = jnp.sum(every[a] * every[b])
            place = ((at_row == a) & (at_lane == b)) | ((at_row == b) & (at_lane == a))
            inner = jnp.where(place, value, inner)
    inner_all[me_p] = inner
    inner_copies = [
        send(inner_all.at[me_p], inner_all.at[me_p], inner_send.at[d], inner_recv.at[d], me_s, peer)
        for d, peer in enumerate(plane_peers)
    ]

    images = velocity[...].reshape(slots * comps * zw, xw)
    columns[...] = jnp.dot(images, shifts, preferred_element_type=jnp.float32)
    lane = lax.broadcasted_iota(jnp.int32, (8, xw), 1)
    group = lax.div(lane, xf)
    weights = {}
    for i in range(comps):
        for f in range(2):
            for a in range(3):
                k = [stencil_ref[i, f, a, b] * (1.0 / (POOL * POOL)) for b in range(3)]
                weights[i, f, a] = jnp.where(group == 0, k[1], jnp.where(group == 1, k[0], k[2]))[:1]
    for slot in range(slots):
        for i in range(comps):
            base = (slot * comps + i) * zw
            part = [columns[pl.ds(base + r, zf, stride=POOL), :] for r in range(POOL)]
            middle = part[1] + part[2]
            sums = [
                shift_rows(part[3], 1) + part[0] + middle,
                part[0] + middle + part[3],
                middle + part[3] + shift_rows(part[0], -1),
            ]
            for f in range(2):
                mixed = sum(weights[i, f, a] * sums[a] for a in range(3))
                mixed = mixed + pltpu.roll(mixed, xw - xf, 1) + pltpu.roll(mixed, xw - 2 * xf, 1)
                feats[slot, pl.ds((2 * i + f) * zf, zf), :] = mixed.astype(jnp.bfloat16)

    stream[...] = jnp.zeros_like(stream)
    stream[pl.ds(xw - xf, xf), :] = stream_ref[...]
    get_table.wait()

    def fold(value):
        return jnp.sum(value.reshape(zf // 8, 8, width), axis=0)

    first_stream = stream[pl.ds(xw - xf, xw), :]
    terms = []
    for slot in range(slots):
        proj = jnp.dot(feats[slot], first_stream, preferred_element_type=jnp.float32)
        block = block_ref[0, slot]
        term = jnp.zeros((8, width), jnp.float32)
        for i in range(comps):
            for f in range(2):
                at = (2 * i + f) * zf
                term = term + fold(proj[at : at + zf] * table[block, 3 * i + f].astype(jnp.float32))
        terms.append(term)

    @pl.when(me_p > 0)
    def _():
        up.wait_recv()

    @pl.when(me_p < planes - 1)
    def _():
        down.wait_recv()

    normals = []
    for slot in range(slots):
        below = halo_in[1] if slot == 0 else pooled[slot - 1]
        above = halo_in[0]
        if slot + 1 < slots:
            above = jnp.where(slot + 1 < live_count, pooled[slot + 1], above)
        scale = span_ref[0, slot] * (1.0 / (POOL * POOL))
        normals.append(((above - below) * scale).astype(jnp.bfloat16))
    normals = jnp.concatenate(normals, axis=0)
    for i in range(comps):
        proj = jnp.dot(
            normals, stream[pl.ds(xw - xf - i * xf, xw), :], preferred_element_type=jnp.float32
        )
        for slot in range(slots):
            at = slot * zf
            tile = table[block_ref[0, slot], 3 * i + 2].astype(jnp.float32)
            terms[slot] = terms[slot] + fold(proj[at : at + zf] * tile)
    total = jnp.zeros((8, width), jnp.float32)
    for slot in range(slots):
        total = total + jnp.where(slot < live_count, terms[slot], 0.0)
    coef_all[me_p] = jnp.sum(total, axis=0, keepdims=True)
    coef_copies = [
        send(coef_all.at[me_p], coef_all.at[me_p], coef_send.at[d], coef_recv.at[d], me_s, peer)
        for d, peer in enumerate(plane_peers)
    ]

    stacked = jnp.concatenate([shear_all[s] for s in range(snaps)], axis=0)
    spare = xw - stacked.shape[0]
    if spare:
        stacked = jnp.concatenate([stacked, jnp.zeros((spare, xw), jnp.float32)], axis=0)
    shear_t[...] = stacked.T
    xl = xf // snaps
    mine = shear_t[pl.ds(me_s * xl, xl), :]
    for copy in inner_copies:
        copy.wait()
    inner = inner_all[0]
    for p in range(1, planes):
        inner = inner + inner_all[p]

    for copy in coef_copies:
        copy.wait()
    coef = coef_all[0]
    for p in range(1, planes):
        coef = coef + coef_all[p]
    coef_snap[me_s] = coef
    snap_copies = [
        send(coef_snap.at[me_s], coef_snap.at[me_s], snap_send.at[d], snap_recv.at[d], peer, me_p)
        for d, peer in enumerate(snap_peers)
    ]
    for copy in snap_copies:
        copy.wait()

    coefs = [coef_snap[s] for s in range(snaps)]
    rows = kinds * zl
    for m in range(kinds):
        for z in range(zl):
            value = jnp.zeros((xl, width), jnp.float32)
            for s in range(snaps):
                at = s * rows + m * zl + z
                value = value + mine[:, at : at + 1] * coefs[s]
            sketch_ref[m, z] = value
    weighted = jnp.zeros((inner_rows, width), jnp.float32)
    for s in range(snaps):
        weighted = weighted + inner[:, s : s + 1] * coefs[s]
    padded = coefs
    if inner_rows > snaps:
        padded = coefs + [jnp.zeros((inner_rows - snaps, width), jnp.float32)]
    stack = jnp.concatenate(padded, axis=0)
    total_rows = kinds * xf * zl * planes
    gram_ref[...] = jnp.dot(
        stack.T, weighted * (1.0 / total_rows), precision=HIGHEST,
        preferred_element_type=jnp.float32,
    )

    @pl.when(me_p > 0)
    def _():
        down.wait_send()

    @pl.when(me_p < planes - 1)
    def _():
        up.wait_send()


def per_device(
    velocity, plane_count, inv_span, kernels, omega_block, omega_table, omega_stream, wall_shear
):
    snaps, planes = lax.axis_size("snap"), lax.axis_size("plane")
    _, slots, comps, zw, xw = velocity.shape
    zf, xf = zw // POOL, xw // POOL
    width = omega_stream.shape[1]
    _, kinds, zs, _ = wall_shear.shape
    zl = zs // POOL
    inner_rows = -(-snaps // 8) * 8
    smem = pl.BlockSpec(memory_space=pltpu.SMEM)
    vmem = pl.BlockSpec(memory_space=pltpu.VMEM)
    hbm = pl.BlockSpec(memory_space=pl.ANY)
    dma = pltpu.SemaphoreType.DMA
    f32, bf16 = jnp.float32, jnp.bfloat16
    return pl.pallas_call(
        functools.partial(kernel, snaps, planes),
        out_shape=(
            jax.ShapeDtypeStruct((kinds, zl, xf // snaps, width), f32),
            jax.ShapeDtypeStruct((width, width), f32),
        ),
        in_specs=[smem, smem, smem, smem, vmem, vmem, hbm, hbm],
        out_specs=(vmem, vmem),
        scratch_shapes=[
            pltpu.VMEM((slots, comps, zw, xw), bf16),
            pltpu.VMEM(omega_table.shape, bf16),
            pltpu.VMEM((2 * xw - xf, width), bf16),
            pltpu.VMEM((slots, zf, xw), f32),
            pltpu.VMEM((slots * comps * zw, xw), f32),
            pltpu.VMEM((slots, 2 * comps * zf, xw), bf16),
            pltpu.VMEM((kinds * zs, xw), f32),
            pltpu.VMEM((snaps, kinds * zl, xw), f32),
            pltpu.VMEM((xw, xw), f32),
            pltpu.VMEM((planes, inner_rows, xw), f32),
            pltpu.VMEM((2, zf, xw), f32),
            pltpu.VMEM((2, zf, xw), f32),
            pltpu.VMEM((planes, 1, width), f32),
            pltpu.VMEM((snaps, 1, width), f32),
            dma((2,)),
            dma((snaps - 1,)), dma((snaps - 1,)),
            dma((planes - 1,)), dma((planes - 1,)),
            dma((2,)), dma((2,)),
            dma((planes - 1,)), dma((planes - 1,)),
            dma((snaps - 1,)), dma((snaps - 1,)),
        ],
        compiler_params=pltpu.CompilerParams(
            collective_id=0, has_side_effects=True, vmem_limit_bytes=24 * 1024 * 1024
        ),
    )(
        plane_count, inv_span, kernels, omega_block, wall_shear, omega_stream, velocity, omega_table
    )


def solution(mesh):
    return jax.shard_map(
        per_device,
        mesh=mesh,
        in_specs=(
            P("snap", "plane", None, None, None),
            P("plane"),
            P("plane", None),
            P(),
            P("plane", None),
            P(),
            P(),
            P("snap", None, "plane", None),
        ),
        out_specs=(P(None, "plane", "snap", None), P()),
        check_vma=False,
    )
```

time: 199 us -> 27.3 us (0.14)
  local copies, waits for them, and re-layouts: 85.9 us -> 7.03 us
  other arithmetic: 39.3 us -> 0 us
  blocking collectives: 31.8 us -> 0 us
  between operations: 22.6 us -> 1.29 us
  Pallas kernels: 0 us -> 18.6 us
  waiting for transfers between devices: 12.3 us -> 0 us
  starting transfers between devices: 4.37 us -> 0 us
  matrix products: 2.22 us -> 0 us
    another operation x8 -> x0, local copies, waits for them, and re-layouts: 83.7 us -> none  [the longest x4 83.6 us: features(): filtered = grads.reshape(snaps, 9, zw // 4, 4, xw // 4, 4).mean(axis=(3, 5))]
    reduce_sum x5 -> x0, other arithmetic: 31.9 us -> none  [the longest x4 31.8 us: features(): filtered = grads.reshape(snaps, 9, zw // 4, 4, xw // 4, 4).mean(axis=(3, 5))]
    pallas_call x0 -> x1, Pallas kernels: none -> 18.6 us  [per_device(): pl.pallas_call(functools.partial(kernel, snaps, planes), out_shape=(jax.S...]
    all_gather x2 -> x0, blocking collectives: 17.6 us -> none  [the longest x1 9.62 us: per_device(): lax.all_gather(shear_f, 'snap', axis=0, tiled=True)]
    psum x1 -> x0, blocking collectives: 14.2 us -> none  [per_device(): coef = lax.psum(coef, 'plane')]
    reduce_scatter x1 -> x0, waiting for transfers between devices: 12.3 us -> none  [per_device(): lax.psum_scatter(partial_sketch, 'snap', scatter_dimension=2, tiled=True)]
    unnamed x14 -> x15, local copies, waits for them, and re-layouts: 0.04 us -> 7.03 us
    another operation x5 -> x0, other arithmetic: 5.48 us -> none  [features(): grads = jnp.stack([first, second, normal], axis=2).reshape(snaps, 9, zw, xw)]
  transfers between devices with their start and end apart: 3 -> 0, of which waited for: 1 -> 0; matrix products, arithmetic and copies ran while one was open for 3% -> 0% of each run, Pallas kernels for 0% -> 0%
where the time goes in v1:
time: 27.3 us; the launch traced here: 26.9 us
  Pallas kernels  18.6 us (68%)
  local copies, waits for them, and re-layouts  7.03 us (26%)
  between operations  1.29 us (5%)
    pallas_call x1, Pallas kernels, per_device(): pl.pallas_call(functools.partial(kernel, snaps, planes), out_shape=(jax.S...  18.6 us
    unnamed x15, local copies, waits for them, and re-layouts  7.03 us

profile of v1, /device:TPU:0, one launch (start us, length us, event | category | flops | bytes accessed | tf_op | source)
XLA Modules:
  0.0 26.9 jit_solution(8918755743540660797)
XLA Ops:
  1.3 0.7 %copy.10.stencil_ref = f32[3,2,3,3]{3,2,1,0:T(4,128)S(1)} copy(f32[3,2,3,3]{3,1,2,0:T(2,128)} %param.11) | data formatting | bytes 432 | tf_op args[3]
  2.0 0.0 copy-start
  2.0 1.3 %copy-done = bf16[8,9,32,256]{3,2,1,0:T(8,128)(2,1)S(1)} copy-done((bf16[8,9,32,256]{3,2,1,0:T(8,128)(2,1)S(1)}, bf16[8,9,32,256]{3,2,1,0:T(8,128)(2,1)}, u32[]{:S(2)}) %copy-start) | copy-done | bytes 1179672
  3.3 0.0 copy-start.1
  3.3 1.0 %copy-done.1 = bf16[1,4,3,128,128]{4,3,2,1,0:T(8,128)(2,1)S(1)} copy-done((bf16[1,4,3,128,128]{4,3,2,1,0:T(8,128)(2,1)S(1)}, bf16[1,4,3,128,128]{4,3,2,1,0:T(8,128)(2,1)}, u32[]{:S(2)}) %copy-start.1) | copy-done | bytes 393240
  4.3 0.0 copy-start.2
  4.3 0.7 %copy-done.2 = bf16[32,256]{1,0:T(8,128)(2,1)S(1)} copy-done((bf16[32,256]{1,0:T(8,128)(2,1)S(1)}, bf16[32,256]{1,0:T(8,128)(2,1)}, u32[]{:S(2)}) %copy-start.2) | copy-done | bytes 16408
  5.0 0.0 copy-start.3
  5.0 0.7 %copy-done.3 = bf16[1,2,16,128]{3,2,1,0:T(8,128)(2,1)S(1)} copy-done((bf16[1,2,16,128]{3,2,1,0:T(8,128)(2,1)S(1)}, bf16[1,2,16,128]{3,2,1,0:T(8,128)(2,1)}, u32[]{:S(2)}) %copy-start.3) | copy-done | bytes 8216
  5.7 0.0 copy-start.4
  5.7 0.7 %copy-done.4 = f32[1,4]{1,0:T(1,128)S(1)} copy-done((f32[1,4]{1,0:T(1,128)S(1)}, f32[1,4]{1,0:T(1,128)}, u32[]{:S(2)}) %copy-start.4) | copy-done | bytes 40
  6.3 0.0 copy-start.5
  6.3 0.7 %copy-done.5 = s32[1,4]{1,0:T(1,128)S(1)} copy-done((s32[1,4]{1,0:T(1,128)S(1)}, s32[1,4]{1,0:T(1,128)}, u32[]{:S(2)}) %copy-start.5) | copy-done | bytes 40
  7.0 18.6 %shard_map.95 = (f32[2,4,8,256]{3,2,1,0:T(8,128)S(1)}, f32[256,256]{1,0:T(8,128)S(1)}) custom-call(s32[1]{0:T(128)S(6)} %copy.13.count_ref, f32[1,4]{1,0:T(1,128)S(1)} %copy-done.4, f32[3,2,3,3]{3,2,1,0:T(4,128)S(1)} %copy.10.stencil_ref, s32[1,4]{1,0:T(1,128)S(1)} %copy-done.5, bf16[1,2,16,128]{3,2,1,0:T(8,128)(2,1)S(1)} %copy-done.3, ...), custom_call_target="tpu_custom_call" | custom-call | tf_op jit(solution)/shard_map/pallas_call | solution.py:291
  25.6 0.6 %copy.14 = f32[2,4,8,256]{3,2,1,0:T(8,128)} copy(f32[2,4,8,256]{3,2,1,0:T(8,128)S(1)} %get-tuple-element.4) | data formatting | bytes 131072
  26.2 0.7 %copy.15 = f32[256,256]{1,0:T(8,128)} copy(f32[256,256]{1,0:T(8,128)S(1)} %get-tuple-element.5) | data formatting | bytes 524288
Async XLA Ops:
  2.0 1.3 %copy-start = (bf16[8,9,32,256]{3,2,1,0:T(8,128)(2,1)S(1)}, bf16[8,9,32,256]{3,2,1,0:T(8,128)(2,1)}, u32[]{:S(2)}) copy-start(bf16[8,9,32,256]{3,2,1,0:T(8,128)(2,1)} %table_hbm.1) | copy-start | bytes 3538948
  3.3 1.0 %copy-start.1 = (bf16[1,4,3,128,128]{4,3,2,1,0:T(8,128)(2,1)S(1)}, bf16[1,4,3,128,128]{4,3,2,1,0:T(8,128)(2,1)}, u32[]{:S(2)}) copy-start(bf16[1,4,3,128,128]{4,3,2,1,0:T(8,128)(2,1)} %velocity_hbm.1) | copy-start | bytes 1179652
  4.3 0.7 %copy-start.2 = (bf16[32,256]{1,0:T(8,128)(2,1)S(1)}, bf16[32,256]{1,0:T(8,128)(2,1)}, u32[]{:S(2)}) copy-start(bf16[32,256]{1,0:T(8,128)(2,1)} %stream_ref.1) | copy-start | bytes 49156
  5.0 0.7 %copy-start.3 = (bf16[1,2,16,128]{3,2,1,0:T(8,128)(2,1)S(1)}, bf16[1,2,16,128]{3,2,1,0:T(8,128)(2,1)}, u32[]{:S(2)}) copy-start(bf16[1,2,16,128]{3,2,1,0:T(8,128)(2,1)} %shear_ref.1) | copy-start | bytes 24580
  5.7 0.7 %copy-start.4 = (f32[1,4]{1,0:T(1,128)S(1)}, f32[1,4]{1,0:T(1,128)}, u32[]{:S(2)}) copy-start(f32[1,4]{1,0:T(1,128)} %span_ref.1) | copy-start | bytes 52
  6.3 0.7 %copy-start.5 = (s32[1,4]{1,0:T(1,128)S(1)}, s32[1,4]{1,0:T(1,128)}, u32[]{:S(2)}) copy-start(s32[1,4]{1,0:T(1,128)} %block_ref.1) | copy-start | bytes 52

commit v2 on v1

--- a/solution.py
+++ b/solution.py
@@ -21,22 +21,17 @@
 
 def kernel(
     snaps, planes,
-    count_ref, span_ref, stencil_ref, block_ref, shear_ref, stream_ref, velocity_hbm, table_hbm,
+    count_hbm, span_hbm, stencil_hbm, block_hbm, shear_hbm, stream_hbm, velocity_hbm, table_hbm,
     sketch_ref, gram_ref,
-    velocity, table, stream, pooled, columns, feats, shear_rows, shear_all, shear_t, inner_all,
+    count_ref, span_ref, stencil_ref, block_ref, shear_ref, stream_ref, velocity, table, stream, pooled, columns, feats, shear_rows, shear_all, shear_t, inner_all,
     halo_out, halo_in, coef_all, coef_snap,
     local_sem, shear_send, shear_recv, inner_send, inner_recv, halo_send, halo_recv,
     coef_send, coef_recv, snap_send, snap_recv,
 ):
     slots, comps, zw, xw = velocity.shape
     zf, xf = zw // POOL, xw // POOL
-    width = stream_ref.shape[1]
+    width = stream_hbm.shape[1]
     me_s, me_p = lax.axis_index("snap"), lax.axis_index("plane")
-
-    get_velocity = pltpu.make_async_copy(velocity_hbm.at[0], velocity, local_sem.at[0])
-    get_table = pltpu.make_async_copy(table_hbm, table, local_sem.at[1])
-    get_velocity.start()
-    get_table.start()
 
     snap_peers = [lax.rem(me_s + d, snaps) for d in range(1, snaps)]
     plane_peers = [lax.rem(me_p + d, planes) for d in range(1, planes)]
@@ -45,6 +40,20 @@
         pl.semaphore_signal(barrier, inc=1, device_id=(peer, me_p), device_id_type=MESH)
     for peer in plane_peers:
         pl.semaphore_signal(barrier, inc=1, device_id=(me_s, peer), device_id_type=MESH)
+
+    def fetch(index, source, target):
+        copy = pltpu.make_async_copy(source, target, local_sem.at[index])
+        copy.start()
+        return copy
+
+    get_velocity = fetch(0, velocity_hbm.at[0], velocity)
+    get_shear = fetch(1, shear_hbm, shear_ref)
+    get_count = fetch(2, count_hbm, count_ref)
+    get_stencil = fetch(3, stencil_hbm, stencil_ref)
+    get_span = fetch(4, span_hbm, span_ref)
+    get_block = fetch(5, block_hbm, block_ref)
+    get_stream = fetch(6, stream_hbm, stream_ref)
+    get_table = fetch(7, table_hbm, table)
 
     row = lax.broadcasted_iota(jnp.int32, (comps * xw, xw), 0)
     lane = lax.broadcasted_iota(jnp.int32, (comps * xw, xw), 1)
@@ -60,12 +69,54 @@
 
     kinds, zs = shear_ref.shape[1], shear_ref.shape[2]
     zl = zs // POOL
+    get_shear.wait()
     shear_in = shear_ref[0].reshape(kinds * zs, xw)
     shear_rows[...] = jnp.dot(shear_in, pack[:xw], preferred_element_type=jnp.float32)
     part = [shear_rows[pl.ds(r, kinds * zl, stride=POOL), :] for r in range(POOL)]
     shear_all[me_s] = (part[0] + part[1] + part[2] + part[3]) * (1.0 / (POOL * POOL))
 
+    get_velocity.wait()
+    fields = jnp.concatenate(
+        [velocity[:, i].reshape(slots * zw, xw) for i in range(comps)], axis=1
+    )
+    columns[pl.ds(0, slots * zw), :] = jnp.dot(fields, pack, preferred_element_type=jnp.float32)
+    part = [columns[pl.ds(r, slots * zf, stride=POOL), :] for r in range(POOL)]
+    pooled[...] = (part[0] + part[1] + part[2] + part[3]).reshape(slots, zf, xw)
+    get_count.wait()
+    live_count = count_ref[0, 0]
+    halo_out[0] = pooled[0]
+    last = pooled[0]
+    for slot in range(1, slots):
+        last = jnp.where(live_count - 1 == slot, pooled[slot], last)
+    halo_out[1] = last
+
     pl.semaphore_wait(barrier, snaps - 1 + planes - 1)
+
+    def halo(which, plane):
+        return pltpu.make_async_remote_copy(
+            src_ref=halo_out.at[which], dst_ref=halo_in.at[which],
+            send_sem=halo_send.at[which], recv_sem=halo_recv.at[which],
+            device_id=(me_s, plane), device_id_type=MESH,
+        )
+
+    down = halo(0, jnp.maximum(me_p - 1, 0))
+    up = halo(1, jnp.minimum(me_p + 1, planes - 1))
+
+    @pl.when(me_p > 0)
+    def _():
+        down.start()
+
+    @pl.when(me_p < planes - 1)
+    def _():
+        up.start()
+
+    @pl.when(me_p == 0)
+    def _():
+        halo_in[1] = jnp.zeros_like(halo_in[1])
+
+    @pl.when(me_p == planes - 1)
+    def _():
+        halo_in[0] = jnp.zeros_like(halo_in[0])
 
     def send(src, dst, send_sem, recv_sem, snap, plane):
         copy = pltpu.make_async_remote_copy(
@@ -80,45 +131,53 @@
         for d, peer in enumerate(snap_peers)
     ]
 
-    get_velocity.wait()
-    fields = jnp.concatenate(
-        [velocity[:, i].reshape(slots * zw, xw) for i in range(comps)], axis=1
-    )
-    columns[pl.ds(0, slots * zw), :] = jnp.dot(fields, pack, preferred_element_type=jnp.float32)
-    part = [columns[pl.ds(r, slots * zf, stride=POOL), :] for r in range(POOL)]
-    pooled[...] = (part[0] + part[1] + part[2] + part[3]).reshape(slots, zf, xw)
-    live_count = count_ref[0]
-    halo_out[0] = pooled[0]
-    last = pooled[0]
-    for slot in range(1, slots):
-        last = jnp.where(live_count - 1 == slot, pooled[slot], last)
-    halo_out[1] = last
-
-    def halo(which, plane):
-        return pltpu.make_async_remote_copy(
-            src_ref=halo_out.at[which], dst_ref=halo_in.at[which],
-            send_sem=halo_send.at[which], recv_sem=halo_recv.at[which],
-            device_id=(me_s, plane), device_id_type=MESH,
-        )
-
-    down = halo(0, jnp.maximum(me_p - 1, 0))
-    up = halo(1, jnp.minimum(me_p + 1, planes - 1))
-
-    @pl.when(me_p > 0)
-    def _():
-        down.start()
-
-    @pl.when(me_p < planes - 1)
-    def _():
-        up.start()
-
-    @pl.when(me_p == 0)
-    def _():
-        halo_in[1] = jnp.zeros_like(halo_in[1])
-
-    @pl.when(me_p == planes - 1)
-    def _():
-        halo_in[0] = jnp.zeros_like(halo_in[0])
+    images = velocity[...].reshape(slots * comps * zw, xw)
+    columns[...] = jnp.dot(images, shifts, preferred_element_type=jnp.float32)
+    lane = lax.broadcasted_iota(jnp.int32, (8, xw), 1)
+    group = lax.div(lane, xf)
+    get_stencil.wait()
+    weights = {}
+    for i in range(comps):
+        for f in range(2):
+            for a in range(3):
+                k = [stencil_ref[i, a, f, b] * (1.0 / (POOL * POOL)) for b in range(3)]
+                weights[i, f, a] = jnp.where(group == 0, k[1], jnp.where(group == 1, k[0], k[2]))[:1]
+    for slot in range(slots):
+        for i in range(comps):
+            base = (slot * comps + i) * zw
+            part = [columns[pl.ds(base + r, zf, stride=POOL), :] for r in range(POOL)]
+            middle = part[1] + part[2]
+            sums = [
+                shift_rows(part[3], 1) + part[0] + middle,
+                part[0] + middle + part[3],
+                middle + part[3] + shift_rows(part[0], -1),
+            ]
+            for f in range(2):
+                mixed = sum(weights[i, f, a] * sums[a] for a in range(3))
+                mixed = mixed + pltpu.roll(mixed, xw - xf, 1) + pltpu.roll(mixed, xw - 2 * xf, 1)
+                feats[slot, pl.ds((2 * i + f) * zf, zf), :] = mixed.astype(jnp.bfloat16)
+
+    stream[...] = jnp.zeros_like(stream)
+    get_stream.wait()
+    stream[pl.ds(xw - xf, xf), :] = stream_ref[...]
+    get_table.wait()
+    get_block.wait()
+    get_span.wait()
+
+    def fold(value):
+        return jnp.sum(value.reshape(zf // 8, 8, width), axis=0)
+
+    first_stream = stream[pl.ds(xw - xf, xw), :]
+    terms = []
+    for slot in range(slots):
+        proj = jnp.dot(feats[slot], first_stream, preferred_element_type=jnp.float32)
+        block = block_ref[0, slot]
+        term = jnp.zeros((8, width), jnp.float32)
+        for i in range(comps):
+            for f in range(2):
+                at = (2 * i + f) * zf
+                term = term + fold(proj[at : at + zf] * table[block, 3 * i + f].astype(jnp.float32))
+        terms.append(term)
 
     for copy in shear_copies:
         copy.wait()
@@ -137,50 +196,6 @@
         send(inner_all.at[me_p], inner_all.at[me_p], inner_send.at[d], inner_recv.at[d], me_s, peer)
         for d, peer in enumerate(plane_peers)
     ]
-
-    images = velocity[...].reshape(slots * comps * zw, xw)
-    columns[...] = jnp.dot(images, shifts, preferred_element_type=jnp.float32)
-    lane = lax.broadcasted_iota(jnp.int32, (8, xw), 1)
-    group = lax.div(lane, xf)
-    weights = {}
-    for i in range(comps):
-        for f in range(2):
-            for a in range(3):
-                k = [stencil_ref[i, f, a, b] * (1.0 / (POOL * POOL)) for b in range(3)]
-                weights[i, f, a] = jnp.where(group == 0, k[1], jnp.where(group == 1, k[0], k[2]))[:1]
-    for slot in range(slots):
-        for i in range(comps):
-            base = (slot * comps + i) * zw
-            part = [columns[pl.ds(base + r, zf, stride=POOL), :] for r in range(POOL)]
-            middle = part[1] + part[2]
-            sums = [
-                shift_rows(part[3], 1) + part[0] + middle,
-                part[0] + middle + part[3],
-                middle + part[3] + shift_rows(part[0], -1),
-            ]
-            for f in range(2):
-                mixed = sum(weights[i, f, a] * sums[a] for a in range(3))
-                mixed = mixed + pltpu.roll(mixed, xw - xf, 1) + pltpu.roll(mixed, xw - 2 * xf, 1)
-                feats[slot, pl.ds((2 * i + f) * zf, zf), :] = mixed.astype(jnp.bfloat16)
-
-    stream[...] = jnp.zeros_like(stream)
-    stream[pl.ds(xw - xf, xf), :] = stream_ref[...]
-    get_table.wait()
-
-    def fold(value):
-        return jnp.sum(value.reshape(zf // 8, 8, width), axis=0)
-
-    first_stream = stream[pl.ds(xw - xf, xw), :]
-    terms = []
-    for slot in range(slots):
-        proj = jnp.dot(feats[slot], first_stream, preferred_element_type=jnp.float32)
-        block = block_ref[0, slot]
-        term = jnp.zeros((8, width), jnp.float32)
-        for i in range(comps):
-            for f in range(2):
-                at = (2 * i + f) * zf
-                term = term + fold(proj[at : at + zf] * table[block, 3 * i + f].astype(jnp.float32))
-        terms.append(term)
 
     @pl.when(me_p > 0)
     def _():
@@ -283,20 +298,27 @@
     _, kinds, zs, _ = wall_shear.shape
     zl = zs // POOL
     inner_rows = -(-snaps // 8) * 8
-    smem = pl.BlockSpec(memory_space=pltpu.SMEM)
     vmem = pl.BlockSpec(memory_space=pltpu.VMEM)
-    hbm = pl.BlockSpec(memory_space=pl.ANY)
+    hbm = pl.BlockSpec(memory_space=pltpu.HBM)
     dma = pltpu.SemaphoreType.DMA
     f32, bf16 = jnp.float32, jnp.bfloat16
+    stencils = kernels.transpose(0, 2, 1, 3)
+    counts = plane_count.reshape(1, -1)
     return pl.pallas_call(
         functools.partial(kernel, snaps, planes),
         out_shape=(
             jax.ShapeDtypeStruct((kinds, zl, xf // snaps, width), f32),
             jax.ShapeDtypeStruct((width, width), f32),
         ),
-        in_specs=[smem, smem, smem, smem, vmem, vmem, hbm, hbm],
+        in_specs=[hbm] * 8,
         out_specs=(vmem, vmem),
         scratch_shapes=[
+            pltpu.SMEM(counts.shape, jnp.int32),
+            pltpu.SMEM(inv_span.shape, f32),
+            pltpu.SMEM(stencils.shape, f32),
+            pltpu.SMEM(omega_block.shape, jnp.int32),
+            pltpu.VMEM(wall_shear.shape, bf16),
+            pltpu.VMEM(omega_stream.shape, bf16),
             pltpu.VMEM((slots, comps, zw, xw), bf16),
             pltpu.VMEM(omega_table.shape, bf16),
             pltpu.VMEM((2 * xw - xf, width), bf16),
@@ -311,7 +333,7 @@
             pltpu.VMEM((2, zf, xw), f32),
             pltpu.VMEM((planes, 1, width), f32),
             pltpu.VMEM((snaps, 1, width), f32),
-            dma((2,)),
+            dma((8,)),
             dma((snaps - 1,)), dma((snaps - 1,)),
             dma((planes - 1,)), dma((planes - 1,)),
             dma((2,)), dma((2,)),
@@ -319,10 +341,10 @@
             dma((snaps - 1,)), dma((snaps - 1,)),
         ],
         compiler_params=pltpu.CompilerParams(
-            collective_id=0, has_side_effects=True, vmem_limit_bytes=24 * 1024 * 1024
+            collective_id=0, has_side_effects=True, vmem_limit_bytes=64 * 1024 * 1024
         ),
     )(
-        plane_count, inv_span, kernels, omega_block, wall_shear, omega_stream, velocity, omega_table
+        counts, inv_span, stencils, omega_block, wall_shear, omega_stream, velocity, omega_table
     )
 
 

time: 27.3 us -> 22.1 us (0.81)
  local copies, waits for them, and re-layouts: 7.03 us -> 3.14 us
  Pallas kernels: 18.6 us -> 17.4 us
    unnamed x15 -> x2, local copies, waits for them, and re-layouts: 7.03 us -> 3.14 us
    pallas_call x1, Pallas kernels: 18.6 us -> 17.4 us  [per_device(): pl.pallas_call(functools.partial(kernel, snaps, planes), out_shape=(jax.S...]
where the time goes in v2:
time: 22.1 us; the launch traced here: 21.8 us
  Pallas kernels  17.4 us (79%)
  local copies, waits for them, and re-layouts  3.14 us (14%)
  between operations  1.29 us (6%)
    pallas_call x1, Pallas kernels, per_device(): pl.pallas_call(functools.partial(kernel, snaps, planes), out_shape=(jax.S...  17.4 us
    unnamed x2, local copies, waits for them, and re-layouts  3.14 us

profile of v2, /device:TPU:0, one launch (start us, length us, event | category | flops | bytes accessed | tf_op | source)
XLA Modules:
  0.0 21.8 jit_solution(5853520540947345513)
XLA Ops:
  1.3 17.4 %shard_map.95 = (f32[2,4,8,256]{3,2,1,0:T(8,128)}, f32[256,256]{1,0:T(8,128)}) custom-call(s32[1,1]{1,0:T(1,128)} %bitcast.2.count_hbm, f32[1,4]{1,0:T(1,128)} %span_hbm.1, f32[3,3,2,3]{3,2,1,0:T(2,128)} %bitcast.3, s32[1,4]{1,0:T(1,128)} %block_hbm.1, bf16[1,2,16,128]{3,2,1,0:T(8,128)(2,1)} %shear_hbm.1, bf16[32,256]{1,0:T(8,128)(2,1)} %stream_hbm.1, ...), custom_call_target="tpu_custom_call" | custom-call | tf_op jit(solution)/shard_map/pallas_call | solution.py:307
  18.7 1.5 %copy.13 = f32[2,4,8,256]{3,2,1,0:T(8,128)} copy(f32[2,4,8,256]{3,2,1,0:T(8,128)} %get-tuple-element.4) | data formatting | bytes 131072
  20.2 1.7 %copy.14 = f32[256,256]{1,0:T(8,128)} copy(f32[256,256]{1,0:T(8,128)} %get-tuple-element.5) | data formatting | bytes 524288

commit v3 on v2

--- a/solution.py
+++ b/solution.py
@@ -21,9 +21,9 @@
 
 def kernel(
     snaps, planes,
-    count_hbm, span_hbm, stencil_hbm, block_hbm, shear_hbm, stream_hbm, velocity_hbm, table_hbm,
-    sketch_ref, gram_ref,
-    count_ref, span_ref, stencil_ref, block_ref, shear_ref, stream_ref, velocity, table, stream, pooled, columns, feats, shear_rows, shear_all, shear_t, inner_all,
+    count_ref, span_hbm, stencil_hbm, block_hbm, shear_hbm, stream_hbm, velocity_hbm, table_hbm,
+    coef_ref, mine_ref, inner_ref,
+    span_ref, stencil_ref, block_ref, shear_ref, stream_ref, velocity, table, stream, pooled, columns, feats, shear_rows, shear_all, shear_t, inner_all,
     halo_out, halo_in, coef_all, coef_snap,
     local_sem, shear_send, shear_recv, inner_send, inner_recv, halo_send, halo_recv,
     coef_send, coef_recv, snap_send, snap_recv,
@@ -48,12 +48,11 @@
 
     get_velocity = fetch(0, velocity_hbm.at[0], velocity)
     get_shear = fetch(1, shear_hbm, shear_ref)
-    get_count = fetch(2, count_hbm, count_ref)
-    get_stencil = fetch(3, stencil_hbm, stencil_ref)
-    get_span = fetch(4, span_hbm, span_ref)
-    get_block = fetch(5, block_hbm, block_ref)
-    get_stream = fetch(6, stream_hbm, stream_ref)
-    get_table = fetch(7, table_hbm, table)
+    get_stencil = fetch(2, stencil_hbm, stencil_ref)
+    get_span = fetch(3, span_hbm, span_ref)
+    get_block = fetch(4, block_hbm, block_ref)
+    get_stream = fetch(5, stream_hbm, stream_ref)
+    get_table = fetch(6, table_hbm, table)
 
     row = lax.broadcasted_iota(jnp.int32, (comps * xw, xw), 0)
     lane = lax.broadcasted_iota(jnp.int32, (comps * xw, xw), 1)
@@ -82,8 +81,7 @@
     columns[pl.ds(0, slots * zw), :] = jnp.dot(fields, pack, preferred_element_type=jnp.float32)
     part = [columns[pl.ds(r, slots * zf, stride=POOL), :] for r in range(POOL)]
     pooled[...] = (part[0] + part[1] + part[2] + part[3]).reshape(slots, zf, xw)
-    get_count.wait()
-    live_count = count_ref[0, 0]
+    live_count = count_ref[0]
     halo_out[0] = pooled[0]
     last = pooled[0]
     for slot in range(1, slots):
@@ -179,24 +177,6 @@
                 term = term + fold(proj[at : at + zf] * table[block, 3 * i + f].astype(jnp.float32))
         terms.append(term)
 
-    for copy in shear_copies:
-        copy.wait()
-    every = shear_all[...]
-    inner_rows = inner_all.shape[1]
-    at_row = lax.broadcasted_iota(jnp.int32, (inner_rows, xw), 0)
-    at_lane = lax.broadcasted_iota(jnp.int32, (inner_rows, xw), 1)
-    inner = jnp.zeros((inner_rows, xw), jnp.float32)
-    for a in range(snaps):
-        for b in range(a, snaps):
-            value = jnp.sum(every[a] * every[b])
-            place = ((at_row == a) & (at_lane == b)) | ((at_row == b) & (at_lane == a))
-            inner = jnp.where(place, value, inner)
-    inner_all[me_p] = inner
-    inner_copies = [
-        send(inner_all.at[me_p], inner_all.at[me_p], inner_send.at[d], inner_recv.at[d], me_s, peer)
-        for d, peer in enumerate(plane_peers)
-    ]
-
     @pl.when(me_p > 0)
     def _():
         up.wait_recv()
@@ -231,19 +211,31 @@
         for d, peer in enumerate(plane_peers)
     ]
 
+    for copy in shear_copies:
+        copy.wait()
+    every = shear_all[...]
+    inner_rows = inner_all.shape[1]
+    at_row = lax.broadcasted_iota(jnp.int32, (inner_rows, xw), 0)
+    at_lane = lax.broadcasted_iota(jnp.int32, (inner_rows, xw), 1)
+    inner = jnp.zeros((inner_rows, xw), jnp.float32)
+    for a in range(snaps):
+        for b in range(a, snaps):
+            value = jnp.sum(every[a] * every[b])
+            place = ((at_row == a) & (at_lane == b)) | ((at_row == b) & (at_lane == a))
+            inner = jnp.where(place, value, inner)
+    inner_all[me_p] = inner
+    inner_copies = [
+        send(inner_all.at[me_p], inner_all.at[me_p], inner_send.at[d], inner_recv.at[d], me_s, peer)
+        for d, peer in enumerate(plane_peers)
+    ]
+
     stacked = jnp.concatenate([shear_all[s] for s in range(snaps)], axis=0)
     spare = xw - stacked.shape[0]
     if spare:
         stacked = jnp.concatenate([stacked, jnp.zeros((spare, xw), jnp.float32)], axis=0)
     shear_t[...] = stacked.T
     xl = xf // snaps
-    mine = shear_t[pl.ds(me_s * xl, xl), :]
-    for copy in inner_copies:
-        copy.wait()
-    inner = inner_all[0]
-    for p in range(1, planes):
-        inner = inner + inner_all[p]
-
+    mine_ref[...] = shear_t[pl.ds(me_s * xl, xl), :]
     for copy in coef_copies:
         copy.wait()
     coef = coef_all[0]
@@ -254,10 +246,34 @@
         send(coef_snap.at[me_s], coef_snap.at[me_s], snap_send.at[d], snap_recv.at[d], peer, me_p)
         for d, peer in enumerate(snap_peers)
     ]
+    for copy in inner_copies:
+        copy.wait()
+    inner = inner_all[0]
+    for p in range(1, planes):
+        inner = inner + inner_all[p]
+
+    inner_ref[...] = inner
     for copy in snap_copies:
         copy.wait()
-
-    coefs = [coef_snap[s] for s in range(snaps)]
+    coef_ref[...] = jnp.concatenate([coef_snap[s] for s in range(snaps)], axis=0)
+
+    @pl.when(me_p > 0)
+    def _():
+        down.wait_send()
+
+    @pl.when(me_p < planes - 1)
+    def _():
+        up.wait_send()
+
+
+def outputs_kernel(
+    planes, coef_ref, mine_ref, inner_ref, sketch_hbm, gram_hbm, sketch_ref, gram_ref, sems
+):
+    snaps, width = coef_ref.shape
+    kinds, zl, xl, _ = sketch_ref.shape
+    inner_rows = inner_ref.shape[0]
+    mine, inner = mine_ref[...], inner_ref[...]
+    coefs = [coef_ref[pl.ds(s, 1), :] for s in range(snaps)]
     rows = kinds * zl
     for m in range(kinds):
         for z in range(zl):
@@ -266,6 +282,8 @@
                 at = s * rows + m * zl + z
                 value = value + mine[:, at : at + 1] * coefs[s]
             sketch_ref[m, z] = value
+    put_sketch = pltpu.make_async_copy(sketch_ref, sketch_hbm, sems.at[0])
+    put_sketch.start()
     weighted = jnp.zeros((inner_rows, width), jnp.float32)
     for s in range(snaps):
         weighted = weighted + inner[:, s : s + 1] * coefs[s]
@@ -273,19 +291,15 @@
     if inner_rows > snaps:
         padded = coefs + [jnp.zeros((inner_rows - snaps, width), jnp.float32)]
     stack = jnp.concatenate(padded, axis=0)
-    total_rows = kinds * xf * zl * planes
+    total_rows = kinds * (xl * snaps) * zl * planes
     gram_ref[...] = jnp.dot(
         stack.T, weighted * (1.0 / total_rows), precision=HIGHEST,
         preferred_element_type=jnp.float32,
     )
-
-    @pl.when(me_p > 0)
-    def _():
-        down.wait_send()
-
-    @pl.when(me_p < planes - 1)
-    def _():
-        up.wait_send()
+    put_gram = pltpu.make_async_copy(gram_ref, gram_hbm, sems.at[1])
+    put_gram.start()
+    put_sketch.wait()
+    put_gram.wait()
 
 
 def per_device(
@@ -303,17 +317,16 @@
     dma = pltpu.SemaphoreType.DMA
     f32, bf16 = jnp.float32, jnp.bfloat16
     stencils = kernels.transpose(0, 2, 1, 3)
-    counts = plane_count.reshape(1, -1)
-    return pl.pallas_call(
+    coef, mine, inner = pl.pallas_call(
         functools.partial(kernel, snaps, planes),
         out_shape=(
-            jax.ShapeDtypeStruct((kinds, zl, xf // snaps, width), f32),
-            jax.ShapeDtypeStruct((width, width), f32),
+            jax.ShapeDtypeStruct((snaps, width), f32),
+            jax.ShapeDtypeStruct((xf // snaps, xw), f32),
+            jax.ShapeDtypeStruct((inner_rows, xw), f32),
         ),
-        in_specs=[hbm] * 8,
-        out_specs=(vmem, vmem),
+        in_specs=[pl.BlockSpec(memory_space=pltpu.SMEM)] + [hbm] * 7,
+        out_specs=(vmem, vmem, vmem),
         scratch_shapes=[
-            pltpu.SMEM(counts.shape, jnp.int32),
             pltpu.SMEM(inv_span.shape, f32),
             pltpu.SMEM(stencils.shape, f32),
             pltpu.SMEM(omega_block.shape, jnp.int32),
@@ -333,7 +346,7 @@
             pltpu.VMEM((2, zf, xw), f32),
             pltpu.VMEM((planes, 1, width), f32),
             pltpu.VMEM((snaps, 1, width), f32),
-            dma((8,)),
+            dma((7,)),
             dma((snaps - 1,)), dma((snaps - 1,)),
             dma((planes - 1,)), dma((planes - 1,)),
             dma((2,)), dma((2,)),
@@ -341,11 +354,27 @@
             dma((snaps - 1,)), dma((snaps - 1,)),
         ],
         compiler_params=pltpu.CompilerParams(
-            collective_id=0, has_side_effects=True, vmem_limit_bytes=64 * 1024 * 1024
+            collective_id=0, has_side_effects=True, vmem_limit_bytes=24 * 1024 * 1024
         ),
     )(
-        counts, inv_span, stencils, omega_block, wall_shear, omega_stream, velocity, omega_table
+        plane_count,
+        *(
+            pltpu.with_memory_space_constraint(value, pltpu.HBM)
+            for value in (
+                inv_span, stencils, omega_block, wall_shear, omega_stream, velocity, omega_table
+            )
+        )
     )
+    sketch_shape = (kinds, zl, xf // snaps, width)
+    return pl.pallas_call(
+        functools.partial(outputs_kernel, planes),
+        out_shape=(pltpu.HBM(sketch_shape, f32), pltpu.HBM((width, width), f32)),
+        in_specs=[vmem] * 3,
+        out_specs=(hbm, hbm),
+        scratch_shapes=[
+            pltpu.VMEM(sketch_shape, f32), pltpu.VMEM((width, width), f32), dma((2,)),
+        ],
+    )(coef, mine, inner)
 
 
 def solution(mesh):

time: 22.1 us -> 19.7 us (0.89)
  local copies, waits for them, and re-layouts: 3.14 us -> 1.77 us
  Pallas kernels: 17.4 us -> 16.5 us
    pallas_call x1, Pallas kernels: 17.4 us -> 14.6 us  [per_device(): pl.pallas_call(functools.partial(kernel, snaps, planes), out_shape=(jax.S...]
    pallas_call x0 -> x1, Pallas kernels: none -> 1.86 us  [per_device(): pl.pallas_call(functools.partial(outputs_kernel, planes), out_shape=(pltp...]
    unnamed x2 -> x6, local copies, waits for them, and re-layouts: 3.14 us -> 1.77 us
where the time goes in v3:
time: 19.7 us; the launch traced here: 19.6 us
  Pallas kernels  16.5 us (84%)
  local copies, waits for them, and re-layouts  1.77 us (9%)
  between operations  1.3 us (7%)
    pallas_call x1, Pallas kernels, per_device(): pl.pallas_call(functools.partial(kernel, snaps, planes), out_shape=(jax.S...  14.6 us
    pallas_call x1, Pallas kernels, per_device(): pl.pallas_call(functools.partial(outputs_kernel, planes), out_shape=(pltp...  1.86 us
    unnamed x6, local copies, waits for them, and re-layouts  1.77 us

profile of v3, /device:TPU:0, one launch (start us, length us, event | category | flops | bytes accessed | tf_op | source)
XLA Modules:
  0.0 19.6 jit_solution(1311862725131376269)
XLA Ops:
  1.3 14.6 %shard_map.95 = (f32[4,256]{1,0:T(4,128)S(1)}, f32[8,128]{1,0:T(8,128)S(1)}, f32[8,128]{1,0:T(8,128)S(1)}) custom-call(s32[1]{0:T(128)S(6)} %copy.10.count_ref, f32[1,4]{1,0:T(1,128)} %span_hbm.1, f32[3,3,2,3]{3,2,1,0:T(2,128)} %bitcast.1, s32[1,4]{1,0:T(1,128)} %block_hbm.1, bf16[1,2,16,128]{3,2,1,0:T(8,128)(2,1)} %shear_hbm.1, bf16[32,256]{1,0:T(8,128)(2,1)} %stream_hbm.1, ...), custom_call_target="tpu_custom_call" | custom-call | tf_op jit(solution)/shard_map/pallas_call | solution.py:320
  15.9 0.0 copy-start
  15.9 0.6 %copy-done = f32[4,256]{1,0:T(4,128)} copy-done((f32[4,256]{1,0:T(4,128)}, f32[4,256]{1,0:T(4,128)S(1)}, u32[]{:S(2)}) %copy-start) | copy-done | bytes 4120
  16.5 0.0 copy-start.1
  16.5 0.6 %copy-done.1 = f32[8,128]{1,0:T(8,128)} copy-done((f32[8,128]{1,0:T(8,128)}, f32[8,128]{1,0:T(8,128)S(1)}, u32[]{:S(2)}) %copy-start.1) | copy-done | bytes 4120
  17.1 0.0 copy-start.2
  17.1 0.6 %copy-done.2 = f32[8,128]{1,0:T(8,128)} copy-done((f32[8,128]{1,0:T(8,128)}, f32[8,128]{1,0:T(8,128)S(1)}, u32[]{:S(2)}) %copy-start.2) | copy-done | bytes 4120
  17.7 1.9 %shard_map.96 = (f32[2,4,8,256]{3,2,1,0:T(8,128)}, f32[256,256]{1,0:T(8,128)}) custom-call(f32[4,256]{1,0:T(4,128)} %copy-done, f32[8,128]{1,0:T(8,128)} %copy-done.1, f32[8,128]{1,0:T(8,128)} %copy-done.2), custom_call_target="tpu_custom_call" | custom-call | tf_op jit(solution)/shard_map/pallas_call | solution.py:369
Async XLA Ops:
  15.9 0.6 %copy-start = (f32[4,256]{1,0:T(4,128)}, f32[4,256]{1,0:T(4,128)S(1)}, u32[]{:S(2)}) copy-start(f32[4,256]{1,0:T(4,128)S(1)} %get-tuple-element.5.coef_ref) | copy-start | bytes 12292
  16.5 0.6 %copy-start.1 = (f32[8,128]{1,0:T(8,128)}, f32[8,128]{1,0:T(8,128)S(1)}, u32[]{:S(2)}) copy-start(f32[8,128]{1,0:T(8,128)S(1)} %get-tuple-element.6.mine_ref) | copy-start | bytes 12292
  17.1 0.6 %copy-start.2 = (f32[8,128]{1,0:T(8,128)}, f32[8,128]{1,0:T(8,128)S(1)}, u32[]{:S(2)}) copy-start(f32[8,128]{1,0:T(8,128)S(1)} %get-tuple-element.7.inner_ref) | copy-start | bytes 12292

commit v4 on v3

--- a/solution.py
+++ b/solution.py
@@ -20,7 +20,7 @@
 
 
 def kernel(
-    snaps, planes,
+    snaps, planes, everyone,
     count_ref, span_hbm, stencil_hbm, block_hbm, shear_hbm, stream_hbm, velocity_hbm, table_hbm,
     coef_ref, mine_ref, inner_ref,
     span_ref, stencil_ref, block_ref, shear_ref, stream_ref, velocity, table, stream, pooled, columns, feats, shear_rows, shear_all, shear_t, inner_all,
@@ -33,14 +33,6 @@
     width = stream_hbm.shape[1]
     me_s, me_p = lax.axis_index("snap"), lax.axis_index("plane")
 
-    snap_peers = [lax.rem(me_s + d, snaps) for d in range(1, snaps)]
-    plane_peers = [lax.rem(me_p + d, planes) for d in range(1, planes)]
-    barrier = pltpu.get_barrier_semaphore()
-    for peer in snap_peers:
-        pl.semaphore_signal(barrier, inc=1, device_id=(peer, me_p), device_id_type=MESH)
-    for peer in plane_peers:
-        pl.semaphore_signal(barrier, inc=1, device_id=(me_s, peer), device_id_type=MESH)
-
     def fetch(index, source, target):
         copy = pltpu.make_async_copy(source, target, local_sem.at[index])
         copy.start()
@@ -48,23 +40,37 @@
 
     get_velocity = fetch(0, velocity_hbm.at[0], velocity)
     get_shear = fetch(1, shear_hbm, shear_ref)
+    snap_peers = [lax.rem(me_s + d, snaps) for d in range(1, snaps)]
+    plane_peers = [lax.rem(me_p + d, planes) for d in range(1, planes)]
+    if everyone:
+        greeted = [
+            (me_s if ds == 0 else snap_peers[ds - 1], me_p if dp == 0 else plane_peers[dp - 1])
+            for dp in range(planes)
+            for ds in range(snaps)
+            if ds + dp > 0
+        ]
+    else:
+        greeted = [(peer, me_p) for peer in snap_peers] + [(me_s, peer) for peer in plane_peers]
+    barrier = pltpu.get_barrier_semaphore()
+    for peer in greeted:
+        pl.semaphore_signal(barrier, inc=1, device_id=peer, device_id_type=MESH)
+
     get_stencil = fetch(2, stencil_hbm, stencil_ref)
     get_span = fetch(3, span_hbm, span_ref)
     get_block = fetch(4, block_hbm, block_ref)
     get_stream = fetch(5, stream_hbm, stream_ref)
     get_table = fetch(6, table_hbm, table)
 
-    row = lax.broadcasted_iota(jnp.int32, (comps * xw, xw), 0)
-    lane = lax.broadcasted_iota(jnp.int32, (comps * xw, xw), 1)
-    gap = lax.rem(row, xw) - POOL * lax.rem(lane, xf)
-    hit = (lax.div(row, xw) == lax.div(lane, xf)) & (gap >= 0) & (gap < POOL)
-    pack = jnp.where(hit, 1.0, 0.0).astype(jnp.bfloat16)
     row = lax.broadcasted_iota(jnp.int32, (xw, xw), 0)
     lane = lax.broadcasted_iota(jnp.int32, (xw, xw), 1)
-    group = lax.div(lane, xf)
-    gap = row - POOL * lax.rem(lane, xf) - jnp.where(group == 1, -1, jnp.where(group == 2, 1, 0))
-    hit = (group < 3) & (gap >= 0) & (gap < POOL)
-    shifts = jnp.where(hit, 1.0, 0.0).astype(jnp.bfloat16)
+
+    def windows(start):
+        gap = row - start
+        return jnp.where((gap >= 0) & (gap < POOL), 1.0, 0.0).astype(jnp.bfloat16)
+
+    pack = jnp.concatenate([windows(POOL * (lane - xf * i)) for i in range(comps)], axis=0)
+    first = jnp.where(lane < xf, 0, jnp.where(lane < 2 * xf, -1 - POOL * xf, 1 - 2 * POOL * xf))
+    shifts = windows(POOL * lane + first)
 
     kinds, zs = shear_ref.shape[1], shear_ref.shape[2]
     zl = zs // POOL
@@ -88,7 +94,7 @@
         last = jnp.where(live_count - 1 == slot, pooled[slot], last)
     halo_out[1] = last
 
-    pl.semaphore_wait(barrier, snaps - 1 + planes - 1)
+    pl.semaphore_wait(barrier, len(greeted))
 
     def halo(which, plane):
         return pltpu.make_async_remote_copy(
@@ -132,14 +138,13 @@
     images = velocity[...].reshape(slots * comps * zw, xw)
     columns[...] = jnp.dot(images, shifts, preferred_element_type=jnp.float32)
     lane = lax.broadcasted_iota(jnp.int32, (8, xw), 1)
-    group = lax.div(lane, xf)
     get_stencil.wait()
     weights = {}
     for i in range(comps):
         for f in range(2):
             for a in range(3):
                 k = [stencil_ref[i, a, f, b] * (1.0 / (POOL * POOL)) for b in range(3)]
-                weights[i, f, a] = jnp.where(group == 0, k[1], jnp.where(group == 1, k[0], k[2]))[:1]
+                weights[i, f, a] = jnp.where(lane < xf, k[1], jnp.where(lane < 2 * xf, k[0], k[2]))[:1]
     for slot in range(slots):
         for i in range(comps):
             base = (slot * comps + i) * zw
@@ -205,24 +210,22 @@
     total = jnp.zeros((8, width), jnp.float32)
     for slot in range(slots):
         total = total + jnp.where(slot < live_count, terms[slot], 0.0)
-    coef_all[me_p] = jnp.sum(total, axis=0, keepdims=True)
+    coef_all[me_s, me_p] = jnp.sum(total, axis=0, keepdims=True)
+    receivers = greeted if everyone else [(me_s, peer) for peer in plane_peers]
+    mine = coef_all.at[me_s, me_p]
     coef_copies = [
-        send(coef_all.at[me_p], coef_all.at[me_p], coef_send.at[d], coef_recv.at[d], me_s, peer)
-        for d, peer in enumerate(plane_peers)
+        send(mine, mine, coef_send.at[d], coef_recv.at[d], *peer)
+        for d, peer in enumerate(receivers)
     ]
 
     for copy in shear_copies:
         copy.wait()
     every = shear_all[...]
-    inner_rows = inner_all.shape[1]
-    at_row = lax.broadcasted_iota(jnp.int32, (inner_rows, xw), 0)
-    at_lane = lax.broadcasted_iota(jnp.int32, (inner_rows, xw), 1)
-    inner = jnp.zeros((inner_rows, xw), jnp.float32)
+    at_lane = lax.broadcasted_iota(jnp.int32, (snaps, xw), 1)
+    inner = jnp.zeros((snaps, xw), jnp.float32)
     for a in range(snaps):
-        for b in range(a, snaps):
-            value = jnp.sum(every[a] * every[b])
-            place = ((at_row == a) & (at_lane == b)) | ((at_row == b) & (at_lane == a))
-            inner = jnp.where(place, value, inner)
+        column = jnp.sum(jnp.sum(every * every[a][None], axis=1), axis=1, keepdims=True)
+        inner = jnp.where(at_lane == a, column, inner)
     inner_all[me_p] = inner
     inner_copies = [
         send(inner_all.at[me_p], inner_all.at[me_p], inner_send.at[d], inner_recv.at[d], me_s, peer)
@@ -236,16 +239,19 @@
     shear_t[...] = stacked.T
     xl = xf // snaps
     mine_ref[...] = shear_t[pl.ds(me_s * xl, xl), :]
-    for copy in coef_copies:
-        copy.wait()
-    coef = coef_all[0]
-    for p in range(1, planes):
-        coef = coef + coef_all[p]
-    coef_snap[me_s] = coef
-    snap_copies = [
-        send(coef_snap.at[me_s], coef_snap.at[me_s], snap_send.at[d], snap_recv.at[d], peer, me_p)
-        for d, peer in enumerate(snap_peers)
-    ]
+    if not everyone:
+        for copy in coef_copies:
+            copy.wait()
+        coef = coef_all[me_s, 0]
+        for p in range(1, planes):
+            coef = coef + coef_all[me_s, p]
+        coef_snap[me_s] = coef
+        coef_copies = [
+            send(
+                coef_snap.at[me_s], coef_snap.at[me_s], snap_send.at[d], snap_recv.at[d], peer, me_p
+            )
+            for d, peer in enumerate(snap_peers)
+        ]
     for copy in inner_copies:
         copy.wait()
     inner = inner_all[0]
@@ -253,9 +259,16 @@
         inner = inner + inner_all[p]
 
     inner_ref[...] = inner
-    for copy in snap_copies:
+    for copy in coef_copies:
         copy.wait()
-    coef_ref[...] = jnp.concatenate([coef_snap[s] for s in range(snaps)], axis=0)
+    if everyone:
+        for s in range(snaps):
+            coef = coef_all[s, 0]
+            for p in range(1, planes):
+                coef = coef + coef_all[s, p]
+            coef_ref[pl.ds(s, 1), :] = coef
+    else:
+        coef_ref[...] = jnp.concatenate([coef_snap[s] for s in range(snaps)], axis=0)
 
     @pl.when(me_p > 0)
     def _():
@@ -271,7 +284,7 @@
 ):
     snaps, width = coef_ref.shape
     kinds, zl, xl, _ = sketch_ref.shape
-    inner_rows = inner_ref.shape[0]
+    padding = -snaps % 8
     mine, inner = mine_ref[...], inner_ref[...]
     coefs = [coef_ref[pl.ds(s, 1), :] for s in range(snaps)]
     rows = kinds * zl
@@ -284,13 +297,13 @@
             sketch_ref[m, z] = value
     put_sketch = pltpu.make_async_copy(sketch_ref, sketch_hbm, sems.at[0])
     put_sketch.start()
-    weighted = jnp.zeros((inner_rows, width), jnp.float32)
+    weighted = jnp.zeros((snaps, width), jnp.float32)
     for s in range(snaps):
         weighted = weighted + inner[:, s : s + 1] * coefs[s]
-    padded = coefs
-    if inner_rows > snaps:
-        padded = coefs + [jnp.zeros((inner_rows - snaps, width), jnp.float32)]
-    stack = jnp.concatenate(padded, axis=0)
+    stack = coef_ref[...]
+    if padding:
+        stack = jnp.concatenate([stack, jnp.zeros((padding, width), jnp.float32)], axis=0)
+        weighted = jnp.concatenate([weighted, jnp.zeros((padding, width), jnp.float32)], axis=0)
     total_rows = kinds * (xl * snaps) * zl * planes
     gram_ref[...] = jnp.dot(
         stack.T, weighted * (1.0 / total_rows), precision=HIGHEST,
@@ -311,18 +324,19 @@
     width = omega_stream.shape[1]
     _, kinds, zs, _ = wall_shear.shape
     zl = zs // POOL
-    inner_rows = -(-snaps // 8) * 8
+    everyone = snaps * planes <= 64
+    receivers = (snaps * planes if everyone else planes) - 1
     vmem = pl.BlockSpec(memory_space=pltpu.VMEM)
     hbm = pl.BlockSpec(memory_space=pltpu.HBM)
     dma = pltpu.SemaphoreType.DMA
     f32, bf16 = jnp.float32, jnp.bfloat16
     stencils = kernels.transpose(0, 2, 1, 3)
     coef, mine, inner = pl.pallas_call(
-        functools.partial(kernel, snaps, planes),
+        functools.partial(kernel, snaps, planes, everyone),
         out_shape=(
             jax.ShapeDtypeStruct((snaps, width), f32),
             jax.ShapeDtypeStruct((xf // snaps, xw), f32),
-            jax.ShapeDtypeStruct((inner_rows, xw), f32),
+            jax.ShapeDtypeStruct((snaps, xw), f32),
         ),
         in_specs=[pl.BlockSpec(memory_space=pltpu.SMEM)] + [hbm] * 7,
         out_specs=(vmem, vmem, vmem),
@@ -341,16 +355,16 @@
             pltpu.VMEM((kinds * zs, xw), f32),
             pltpu.VMEM((snaps, kinds * zl, xw), f32),
             pltpu.VMEM((xw, xw), f32),
-            pltpu.VMEM((planes, inner_rows, xw), f32),
+            pltpu.VMEM((planes, snaps, xw), f32),
             pltpu.VMEM((2, zf, xw), f32),
             pltpu.VMEM((2, zf, xw), f32),
-            pltpu.VMEM((planes, 1, width), f32),
+            pltpu.VMEM((snaps, planes, 1, width), f32),
             pltpu.VMEM((snaps, 1, width), f32),
             dma((7,)),
             dma((snaps - 1,)), dma((snaps - 1,)),
             dma((planes - 1,)), dma((planes - 1,)),
             dma((2,)), dma((2,)),
-            dma((planes - 1,)), dma((planes - 1,)),
+            dma((receivers,)), dma((receivers,)),
             dma((snaps - 1,)), dma((snaps - 1,)),
         ],
         compiler_params=pltpu.CompilerParams(
@@ -374,6 +388,7 @@
         scratch_shapes=[
             pltpu.VMEM(sketch_shape, f32), pltpu.VMEM((width, width), f32), dma((2,)),
         ],
+        compiler_params=pltpu.CompilerParams(vmem_limit_bytes=16 * 1024 * 1024),
     )(coef, mine, inner)
 
 

time: 19.7 us -> 16.2 us (0.82)
  local copies, waits for them, and re-layouts: 1.77 us -> 0 us
  Pallas kernels: 16.5 us -> 14.8 us
    unnamed x6 -> x0, local copies, waits for them, and re-layouts: 1.77 us -> none
    pallas_call x1, Pallas kernels: 14.6 us -> 13.6 us  [per_device(): pl.pallas_call(functools.partial(kernel, snaps, planes, everyone), out_sh...]
    pallas_call x1, Pallas kernels: 1.86 us -> 1.16 us  [per_device(): pl.pallas_call(functools.partial(outputs_kernel, planes), out_shape=(pltp...]
where the time goes in v4:
time: 16.2 us; the launch traced here: 16.1 us
  Pallas kernels  14.8 us (91%)
  between operations  1.29 us (8%)
    pallas_call x1, Pallas kernels, per_device(): pl.pallas_call(functools.partial(kernel, snaps, planes, everyone), out_sh...  13.6 us
    pallas_call x1, Pallas kernels, per_device(): pl.pallas_call(functools.partial(outputs_kernel, planes), out_shape=(pltp...  1.16 us

profile of v4, /device:TPU:0, one launch (start us, length us, event | category | flops | bytes accessed | tf_op | source)
XLA Modules:
  0.0 16.1 jit_solution(11182905882001708909)
XLA Ops:
  1.3 13.6 %shard_map.95 = (f32[4,256]{1,0:T(4,128)S(1)}, f32[8,128]{1,0:T(8,128)S(1)}, f32[4,128]{1,0:T(4,128)S(1)}) custom-call(s32[1]{0:T(128)S(6)} %copy.10.count_ref, f32[1,4]{1,0:T(1,128)} %span_hbm.1, f32[3,3,2,3]{3,2,1,0:T(2,128)} %bitcast.1, s32[1,4]{1,0:T(1,128)} %block_hbm.1, bf16[1,2,16,128]{3,2,1,0:T(8,128)(2,1)} %shear_hbm.1, bf16[32,256]{1,0:T(8,128)(2,1)} %stream_hbm.1, ...), custom_call_target="tpu_custom_call" | custom-call | tf_op jit(solution)/shard_map/pallas_call | solution.py:334
  14.9 1.2 %shard_map.96 = (f32[2,4,8,256]{3,2,1,0:T(8,128)}, f32[256,256]{1,0:T(8,128)}) custom-call(f32[4,256]{1,0:T(4,128)S(1)} %get-tuple-element.5.coef_ref, f32[8,128]{1,0:T(8,128)S(1)} %get-tuple-element.6.mine_ref, f32[4,128]{1,0:T(4,128)S(1)} %get-tuple-element.7.inner_ref), custom_call_target="tpu_custom_call" | custom-call | tf_op jit(solution)/shard_map/pallas_call | solution.py:383

commit v5 on v4

--- a/solution.py
+++ b/solution.py
@@ -72,14 +72,6 @@
     first = jnp.where(lane < xf, 0, jnp.where(lane < 2 * xf, -1 - POOL * xf, 1 - 2 * POOL * xf))
     shifts = windows(POOL * lane + first)
 
-    kinds, zs = shear_ref.shape[1], shear_ref.shape[2]
-    zl = zs // POOL
-    get_shear.wait()
-    shear_in = shear_ref[0].reshape(kinds * zs, xw)
-    shear_rows[...] = jnp.dot(shear_in, pack[:xw], preferred_element_type=jnp.float32)
-    part = [shear_rows[pl.ds(r, kinds * zl, stride=POOL), :] for r in range(POOL)]
-    shear_all[me_s] = (part[0] + part[1] + part[2] + part[3]) * (1.0 / (POOL * POOL))
-
     get_velocity.wait()
     fields = jnp.concatenate(
         [velocity[:, i].reshape(slots * zw, xw) for i in range(comps)], axis=1
@@ -121,6 +113,14 @@
     @pl.when(me_p == planes - 1)
     def _():
         halo_in[0] = jnp.zeros_like(halo_in[0])
+
+    kinds, zs = shear_ref.shape[1], shear_ref.shape[2]
+    zl = zs // POOL
+    get_shear.wait()
+    shear_in = shear_ref[0].reshape(kinds * zs, xw)
+    shear_rows[...] = jnp.dot(shear_in, pack[:xw], preferred_element_type=jnp.float32)
+    part = [shear_rows[pl.ds(r, kinds * zl, stride=POOL), :] for r in range(POOL)]
+    shear_all[me_s] = (part[0] + part[1] + part[2] + part[3]) * (1.0 / (POOL * POOL))
 
     def send(src, dst, send_sem, recv_sem, snap, plane):
         copy = pltpu.make_async_remote_copy(
@@ -210,11 +210,14 @@
     total = jnp.zeros((8, width), jnp.float32)
     for slot in range(slots):
         total = total + jnp.where(slot < live_count, terms[slot], 0.0)
-    coef_all[me_s, me_p] = jnp.sum(total, axis=0, keepdims=True)
+    slot_of_mine = me_s * planes + me_p
+    coef_all[slot_of_mine] = jnp.sum(total, axis=0, keepdims=True)
     receivers = greeted if everyone else [(me_s, peer) for peer in plane_peers]
-    mine = coef_all.at[me_s, me_p]
+    mine = coef_all.at[slot_of_mine]
     coef_copies = [
-        send(mine, mine, coef_send.at[d], coef_recv.at[d], *peer)
+        send(
+            mine, mine, coef_send.at[0 if everyone else d], coef_recv.at[0 if everyone else d], *peer
+        )
         for d, peer in enumerate(receivers)
     ]
 
@@ -242,9 +245,9 @@
     if not everyone:
         for copy in coef_copies:
             copy.wait()
-        coef = coef_all[me_s, 0]
+        coef = coef_all[me_s * planes]
         for p in range(1, planes):
-            coef = coef + coef_all[me_s, p]
+            coef = coef + coef_all[me_s * planes + p]
         coef_snap[me_s] = coef
         coef_copies = [
             send(
@@ -259,15 +262,18 @@
         inner = inner + inner_all[p]
 
     inner_ref[...] = inner
-    for copy in coef_copies:
-        copy.wait()
     if everyone:
+        several = coef_all.at[pl.ds(0, len(receivers))]
+        pltpu.make_async_copy(several, several, coef_send.at[0]).wait()
+        pltpu.make_async_copy(several, several, coef_recv.at[0]).wait()
         for s in range(snaps):
-            coef = coef_all[s, 0]
+            coef = coef_all[s * planes]
             for p in range(1, planes):
-                coef = coef + coef_all[s, p]
+                coef = coef + coef_all[s * planes + p]
             coef_ref[pl.ds(s, 1), :] = coef
     else:
+        for copy in coef_copies:
+            copy.wait()
         coef_ref[...] = jnp.concatenate([coef_snap[s] for s in range(snaps)], axis=0)
 
     @pl.when(me_p > 0)
@@ -358,13 +364,13 @@
             pltpu.VMEM((planes, snaps, xw), f32),
             pltpu.VMEM((2, zf, xw), f32),
             pltpu.VMEM((2, zf, xw), f32),
-            pltpu.VMEM((snaps, planes, 1, width), f32),
+            pltpu.VMEM((snaps * planes, 1, width), f32),
             pltpu.VMEM((snaps, 1, width), f32),
             dma((7,)),
             dma((snaps - 1,)), dma((snaps - 1,)),
             dma((planes - 1,)), dma((planes - 1,)),
             dma((2,)), dma((2,)),
-            dma((receivers,)), dma((receivers,)),
+            dma((1 if everyone else receivers,)), dma((1 if everyone else receivers,)),
             dma((snaps - 1,)), dma((snaps - 1,)),
         ],
         compiler_params=pltpu.CompilerParams(

time: 16.2 us -> 15.6 us (0.963)
  Pallas kernels: 14.8 us -> 14.2 us
    pallas_call x1, Pallas kernels: 13.6 us -> 13 us  [per_device(): pl.pallas_call(functools.partial(kernel, snaps, planes, everyone), out_sh...]
where the time goes in v5:
time: 15.6 us; the launch traced here: 15.5 us
  Pallas kernels  14.2 us (91%)
  between operations  1.29 us (8%)
    pallas_call x1, Pallas kernels, per_device(): pl.pallas_call(functools.partial(kernel, snaps, planes, everyone), out_sh...  13 us
    pallas_call x1, Pallas kernels, per_device(): pl.pallas_call(functools.partial(outputs_kernel, planes), out_shape=(pltp...  1.16 us

profile of v5, /device:TPU:0, one launch (start us, length us, event | category | flops | bytes accessed | tf_op | source)
XLA Modules:
  0.0 15.5 jit_solution(7436427380684153682)
XLA Ops:
  1.3 13.0 %shard_map.95 = (f32[4,256]{1,0:T(4,128)S(1)}, f32[8,128]{1,0:T(8,128)S(1)}, f32[4,128]{1,0:T(4,128)S(1)}) custom-call(s32[1]{0:T(128)S(6)} %copy.10.count_ref, f32[1,4]{1,0:T(1,128)} %span_hbm.1, f32[3,3,2,3]{3,2,1,0:T(2,128)} %bitcast.1, s32[1,4]{1,0:T(1,128)} %block_hbm.1, bf16[1,2,16,128]{3,2,1,0:T(8,128)(2,1)} %shear_hbm.1, bf16[32,256]{1,0:T(8,128)(2,1)} %stream_hbm.1, ...), custom_call_target="tpu_custom_call" | custom-call | tf_op jit(solution)/shard_map/pallas_call | solution.py:340
  14.3 1.2 %shard_map.96 = (f32[2,4,8,256]{3,2,1,0:T(8,128)}, f32[256,256]{1,0:T(8,128)}) custom-call(f32[4,256]{1,0:T(4,128)S(1)} %get-tuple-element.5.coef_ref, f32[8,128]{1,0:T(8,128)S(1)} %get-tuple-element.6.mine_ref, f32[4,128]{1,0:T(4,128)S(1)} %get-tuple-element.7.inner_ref), custom_call_target="tpu_custom_call" | custom-call | tf_op jit(solution)/shard_map/pallas_call | solution.py:389
